TPU v7x, 32 devices: a whole 2x2x4 slice. The times are simulated.
32 devices in a mesh: groups: 2 (over y), sector: 16 (over z, x, core).
Axes of the slice: x: 2, y: 2, z: 4, core: 2. Of those that a mesh axis runs over, the one named last changes fastest.
Arguments:
- psi: bfloat16 [512, 128, 128], P(('groups', 'sector')), parts along dimension 0, may hold values from -6 to 6
- left_env: bfloat16 [32, 30, 128, 128], P(('groups', 'sector')), parts along dimension 0, may hold values from -0.5 to 0.5
- right_env: bfloat16 [32, 30, 128, 128], P(('groups', 'sector')), parts along dimension 0, may hold values from -0.09375 to 0.09375
- mpo: bfloat16 [32, 30, 30], P('groups'), parts along dimension 0, may hold values from -1 to 1
- block_target: int32 [512, 1], P(('groups', 'sector')), parts along dimension 0, may hold values from 0 to 7; in each aligned block of 16 rows (0 to 15, 16 to 31, ...) at most 2 rows name the same one
- block_phys: int32 [512], P(('groups', 'sector')), parts along dimension 0, may hold values from 0 to 15
Outputs:
- hpsi: bfloat16 [512, 128, 128], P(('groups', 'sector')), parts along dimension 0
There are 2 independent parts, one for each index of `groups`. A program takes and returns all parts, laid end to end along the dimension named above; each array names one. Nothing has to cross between parts.
Inputs may be any that keep to these rules, and one draw needn't show every extreme that they name: `block_target`: among the 16 blocks of one left sector, no offset is named by more than 2 blocks.
All inputs are finite; a program needn't handle non-finite values.
Results may differ from a plain program's by a relative error of at most 0.0057.
Values may be sent and summed in bfloat16 or wider, within the bound.
A program may use at most 192 MiB of HBM per device.

v0:
```python
import jax
import jax.numpy as jnp
from jax import lax
from jax.sharding import PartitionSpec as P

SPREAD = 8


def passed_along(value, axis, steps):
    count = lax.axis_size(axis)
    pairs = [(source, (source + steps) % count) for source in range(count)]
    return lax.ppermute(value, axis, pairs)


def per_device(psi, left_env, right_env, mpo, block_target, block_phys):
    nblock = psi.shape[0]
    width = psi.shape[1]
    bond = left_env.shape[1]
    labels = mpo.shape[0]
    spread = SPREAD
    contracted = jnp.einsum(
        "wab,kbc->kwac", left_env[0], psi, preferred_element_type=jnp.float32
    ).astype(jnp.bfloat16)
    label_hot = (block_phys[:, None] == jnp.arange(labels, dtype=jnp.int32)[None, :]).astype(
        jnp.bfloat16
    )
    picked = jnp.dot(
        label_hot, mpo.reshape(labels, bond * bond), preferred_element_type=jnp.float32
    )
    picked = picked.astype(jnp.bfloat16).reshape(nblock, bond, bond)
    mixed = jnp.einsum(
        "kwac,kwv->kavc", contracted, picked, preferred_element_type=jnp.float32
    ).astype(jnp.bfloat16)
    mixed = mixed.reshape(nblock, width, bond * width)
    offsets = block_target[:, 0]
    right_flat = right_env[0].reshape(bond * width, width)
    gathered = []
    for offset in range(spread):
        if offset == 0:
            gathered.append(right_flat)
        else:
            fetched = passed_along(right_env, "sector", -offset)
            gathered.append(fetched[0].reshape(bond * width, width))
    stacked = jnp.stack(gathered, axis=0)
    offset_hot = (offsets[:, None] == jnp.arange(spread, dtype=jnp.int32)[None, :]).astype(
        jnp.bfloat16
    )
    chosen = jnp.einsum(
        "ko,oxb->kxb", offset_hot, stacked, preferred_element_type=jnp.float32
    ).astype(jnp.bfloat16)
    result = jnp.einsum("kax,kxb->kab", mixed, chosen, preferred_element_type=jnp.float32)
    return result.astype(jnp.bfloat16)


def solution(mesh):
    in_specs = (
        P(("groups", "sector"), None, None),
        P(("groups", "sector"), None, None, None),
        P(("groups", "sector"), None, None, None),
        P("groups", None, None),
        P(("groups", "sector"), None),
        P(("groups", "sector")),
    )
    out_specs = P(("groups", "sector"), None, None)
    return jax.shard_map(
        per_device, mesh=mesh, in_specs=in_specs, out_specs=out_specs, check_vma=False
    )
```

profile of v0, /device:TPU:1, one launch (start us, length us, event | category | flops | bytes accessed | tf_op | source)
XLA Modules:
  0.0 227.4 jit_solution(18156049453859974575)
XLA Ops:
  0.0 0.0 copy-start
  0.0 0.1 collective-permute-start
  0.1 5.7 %collective-permute-start.1 = (bf16[1,30,128,128]{3,2,1,0:T(8,128)(2,1)}, bf16[1,30,128,128]{3,2,1,0:T(8,128)(2,1)}, u32[]{:S(2)}, u32[]{:S(2)}) collective-permute-start(bf16[1,30,128,128]{3,2,1,0:T(8,128)(2,1)} %param.8), channel_id=1, source_target_pairs={{0,14},{1,15},{2,0},{3,1},{4,2},{5,3},{6,4},{7,5},{8,6},{9,7},{10,... | collective-permute-start | bytes 2949128 | tf_op jit(solution)/shard_map/ppermute | solution.py:12
  5.8 1.2 collective-permute-start.2
  7.0 0.2 collective-permute-start.3
  7.2 0.0 collective-permute-start.4
  7.2 0.0 copy-done
  7.2 8.8 %fusion.9 = bf16[16,128,30,128]{3,1,2,0:T(8,128)(2,1)} fusion(bf16[1,30,128,128]{3,2,1,0:T(8,128)(2,1)S(1)} %copy-done, bf16[16,128,128]{2,1,0:T(8,128)(2,1)} %param.6), kind=kOutput, calls=%fused_computation.10 | convolution fusion | flops 2013265920 | bytes 17235968 | tf_op jit(solution)/shard_map/wab,kbc->kwac/dot_general | solution.py:21
  16.0 0.0 copy-start.3
  16.0 0.0 copy-start.4
  16.0 24.5 %copy.13 = bf16[16,128,30,128]{1,2,3,0:T(8,128)(2,1)} copy(bf16[16,128,30,128]{3,1,2,0:T(8,128)(2,1)} %fusion.9) | data formatting | bytes 31457280 | tf_op jit(solution)/shard_map/wab,kbc->kwac/dot_general | solution.py:21
  40.5 0.0 copy-done.3
  40.5 0.2 reshape.10
  40.7 0.0 copy-done.4
  40.7 0.2 convolution_convert_fusion
  40.9 0.3 reshape.11
  41.3 0.0 copy-start.2
  41.3 11.6 %convert_bitcast_fusion = bf16[16,128,30,128]{3,2,1,0:T(8,128)(2,1)} fusion(bf16[16,128,30,128]{1,2,3,0:T(8,128)(2,1)} %copy.13, bf16[16,30,30]{2,1,0:T(8,128)(2,1)S(1)} %reshape.11), kind=kOutput, calls=%fused_computation.3 | convolution fusion | flops 479723520 | bytes 31486080 | tf_op jit(solution)/shard_map/kwac,kwv->kavc/dot_general | solution.py:31
  52.9 0.0 copy-done.2
  52.9 1.0 constant_dynamic-update-slice_fusion.7
  53.9 24.4 %copy.10 = bf16[16,128,30,128]{1,3,2,0:T(8,128)(2,1)} copy(bf16[16,128,30,128]{3,2,1,0:T(8,128)(2,1)} %convert_bitcast_fusion) | data formatting | bytes 31457280 | tf_op jit(solution)/shard_map/convert_element_type | solution.py:33
  78.3 0.0 copy-start.5
  78.3 0.0 collective-permute-done
  78.3 2.6 %collective-permute-start.5 = (bf16[1,30,128,128]{3,2,1,0:T(8,128)(2,1)S(1)}, bf16[1,30,128,128]{3,2,1,0:T(8,128)(2,1)S(1)}, u32[]{:S(2)}, u32[]{:S(2)}) collective-permute-start(bf16[1,30,128,128]{3,2,1,0:T(8,128)(2,1)S(1)} %copy-done.2), channel_id=1, source_target_pairs={{0,10},{1,11},{2,12},{3,13},{4,14},{5,15},{6,0},{7,1},{8,2},{9,3},... | collective-permute-start | bytes 2949128 | tf_op jit(solution)/shard_map/ppermute | solution.py:12
  80.9 2.2 constant_dynamic-update-slice_fusion.6
  83.1 0.0 collective-permute-done.1
  83.1 1.1 collective-permute-start.6
  84.2 2.3 constant_dynamic-update-slice_fusion.5
  86.4 0.0 collective-permute-done.2
  86.4 2.2 constant_dynamic-update-slice_fusion.4
  88.6 0.0 collective-permute-done.3
  88.6 1.0 constant_dynamic-update-slice_fusion.3
  89.7 1.2 collective-permute-done.4
  90.9 1.0 constant_dynamic-update-slice_fusion.2
  91.9 19.9 %collective-permute-done.5 = bf16[1,30,128,128]{3,2,1,0:T(8,128)(2,1)S(1)} collective-permute-done((bf16[1,30,128,128]{3,2,1,0:T(8,128)(2,1)S(1)}, bf16[1,30,128,128]{3,2,1,0:T(8,128)(2,1)S(1)}, u32[]{:S(2)}, u32[]{:S(2)}) %collective-permute-start.5) | collective-permute-done | bytes 983072 | tf_op jit(solution)/shard_map/ppermute | solution.py:12
  111.8 1.0 constant_dynamic-update-slice_fusion.1
  112.9 82.7 %collective-permute-done.6 = bf16[1,30,128,128]{3,2,1,0:T(8,128)(2,1)S(1)} collective-permute-done((bf16[1,30,128,128]{3,2,1,0:T(8,128)(2,1)S(1)}, bf16[1,30,128,128]{3,2,1,0:T(8,128)(2,1)S(1)}, u32[]{:S(2)}, u32[]{:S(2)}) %collective-permute-start.6) | collective-permute-done | bytes 983072 | tf_op jit(solution)/shard_map/ppermute | solution.py:12
  195.6 1.0 constant_dynamic-update-slice_fusion
  196.6 0.0 copy-done.5
  196.6 15.8 %fusion.6 = bf16[16,3840,128]{2,0,1:T(8,128)(2,1)} fusion(bf16[8,3840,128]{2,1,0:T(8,128)(2,1)} %constant_dynamic-update-slice_fusion, s32[16]{0:T(128)S(1)} %bitcast.42), kind=kOutput, calls=%fused_computation.6 | convolution fusion | flops 125829248 | bytes 23593024 | tf_op jit(solution)/shard_map/ko,oxb->kxb/dot_general | solution.py:48
  212.4 0.0 copy-start.1
  212.4 15.0 %fusion.8 = bf16[16,128,128]{2,1,0:T(8,128)(2,1)} fusion(bf16[16,128,3840]{1,2,0:T(8,128)(2,1)} %bitcast.36, bf16[16,3840,128]{2,0,1:T(8,128)(2,1)} %fusion.6), kind=kOutput, calls=%fused_computation.8 | convolution fusion | flops 2013528064 | bytes 31981568 | tf_op jit(solution)/shard_map/kax,kxb->kab/dot_general | solution.py:51
  227.4 0.0 copy-done.1
  (1 shorter events, 0.0 us)
Async XLA Ops:
  0.0 7.2 %copy-start = (bf16[1,30,128,128]{3,2,1,0:T(8,128)(2,1)S(1)}, bf16[1,30,128,128]{3,2,1,0:T(8,128)(2,1)}, u32[]{:S(2)}) copy-start(bf16[1,30,128,128]{3,2,1,0:T(8,128)(2,1)} %param.7) | copy-start | bytes 2949124
  0.0 78.3 %collective-permute-start = (bf16[1,30,128,128]{3,2,1,0:T(8,128)(2,1)}, bf16[1,30,128,128]{3,2,1,0:T(8,128)(2,1)}, u32[]{:S(2)}, u32[]{:S(2)}) collective-permute-start(bf16[1,30,128,128]{3,2,1,0:T(8,128)(2,1)} %param.8), channel_id=1, source_target_pairs={{0,15},{1,0},{2,1},{3,2},{4,3},{5,4},{6,5},{7,6},{8,7},{9,8},{10,9... | collective-permute-start | bytes 2949128 | tf_op jit(solution)/shard_map/ppermute | solution.py:12
  0.1 83.0 %collective-permute-start.1 = (bf16[1,30,128,128]{3,2,1,0:T(8,128)(2,1)}, bf16[1,30,128,128]{3,2,1,0:T(8,128)(2,1)}, u32[]{:S(2)}, u32[]{:S(2)}) collective-permute-start(bf16[1,30,128,128]{3,2,1,0:T(8,128)(2,1)} %param.8), channel_id=1, source_target_pairs={{0,14},{1,15},{2,0},{3,1},{4,2},{5,3},{6,4},{7,5},{8,6},{9,7},{10,... | collective-permute-start | bytes 2949128 | tf_op jit(solution)/shard_map/ppermute | solution.py:12
  5.8 80.7 %collective-permute-start.2 = (bf16[1,30,128,128]{3,2,1,0:T(8,128)(2,1)}, bf16[1,30,128,128]{3,2,1,0:T(8,128)(2,1)}, u32[]{:S(2)}, u32[]{:S(2)}) collective-permute-start(bf16[1,30,128,128]{3,2,1,0:T(8,128)(2,1)} %param.8), channel_id=1, source_target_pairs={{0,13},{1,14},{2,15},{3,0},{4,1},{5,2},{6,3},{7,4},{8,5},{9,6},{10... | collective-permute-start | bytes 2949128 | tf_op jit(solution)/shard_map/ppermute | solution.py:12
  7.0 81.6 %collective-permute-start.3 = (bf16[1,30,128,128]{3,2,1,0:T(8,128)(2,1)}, bf16[1,30,128,128]{3,2,1,0:T(8,128)(2,1)S(1)}, u32[]{:S(2)}, u32[]{:S(2)}) collective-permute-start(bf16[1,30,128,128]{3,2,1,0:T(8,128)(2,1)} %param.8), channel_id=1, source_target_pairs={{0,12},{1,13},{2,14},{3,15},{4,0},{5,1},{6,2},{7,3},{8,4},{9,5},{1... | collective-permute-start | bytes 2949128 | tf_op jit(solution)/shard_map/ppermute | solution.py:12
  7.2 83.7 %collective-permute-start.4 = (bf16[1,30,128,128]{3,2,1,0:T(8,128)(2,1)}, bf16[1,30,128,128]{3,2,1,0:T(8,128)(2,1)S(1)}, u32[]{:S(2)}, u32[]{:S(2)}) collective-permute-start(bf16[1,30,128,128]{3,2,1,0:T(8,128)(2,1)} %param.8), channel_id=1, source_target_pairs={{0,11},{1,12},{2,13},{3,14},{4,15},{5,0},{6,1},{7,2},{8,3},{9,4},{... | collective-permute-start | bytes 2949128 | tf_op jit(solution)/shard_map/ppermute | solution.py:12
  16.0 24.5 %copy-start.3 = (bf16[16,30,30]{2,0,1:T(8,128)(2,1)S(1)}, bf16[16,30,30]{2,0,1:T(8,128)(2,1)}, u32[]{:S(2)}) copy-start(bf16[16,30,30]{2,0,1:T(8,128)(2,1)} %param.9) | copy-start | bytes 86404
  16.0 24.7 %copy-start.4 = (s32[16]{0:T(128)S(1)}, s32[16]{0:T(128)}, u32[]{:S(2)}) copy-start(s32[16]{0:T(128)} %param.11) | copy-start | bytes 196
  41.3 11.6 %copy-start.2 = (bf16[1,30,128,128]{3,2,1,0:T(8,128)(2,1)S(1)}, bf16[1,30,128,128]{3,2,1,0:T(8,128)(2,1)}, u32[]{:S(2)}) copy-start(bf16[1,30,128,128]{3,2,1,0:T(8,128)(2,1)} %param.8) | copy-start | bytes 2949124
  78.3 118.3 %copy-start.5 = (s32[16,1]{0,1:T(1,128)S(1)}, s32[16,1]{0,1:T(1,128)}, u32[]{:S(2)}) copy-start(s32[16,1]{0,1:T(1,128)} %param.10) | copy-start | bytes 196
  78.3 33.6 %collective-permute-start.5 = (bf16[1,30,128,128]{3,2,1,0:T(8,128)(2,1)S(1)}, bf16[1,30,128,128]{3,2,1,0:T(8,128)(2,1)S(1)}, u32[]{:S(2)}, u32[]{:S(2)}) collective-permute-start(bf16[1,30,128,128]{3,2,1,0:T(8,128)(2,1)S(1)} %copy-done.2), channel_id=1, source_target_pairs={{0,10},{1,11},{2,12},{3,13},{4,14},{5,15},{6,0},{7,1},{8,2},{9,3},... | collective-permute-start | bytes 2949128 | tf_op jit(solution)/shard_map/ppermute | solution.py:12
  83.1 112.5 %collective-permute-start.6 = (bf16[1,30,128,128]{3,2,1,0:T(8,128)(2,1)S(1)}, bf16[1,30,128,128]{3,2,1,0:T(8,128)(2,1)S(1)}, u32[]{:S(2)}, u32[]{:S(2)}) collective-permute-start(bf16[1,30,128,128]{3,2,1,0:T(8,128)(2,1)S(1)} %copy-done.2), channel_id=1, source_target_pairs={{0,9},{1,10},{2,11},{3,12},{4,13},{5,14},{6,15},{7,0},{8,1},{9,2},... | collective-permute-start | bytes 2949128 | tf_op jit(solution)/shard_map/ppermute | solution.py:12
  212.4 15.0 %copy-start.1 = (bf16[1,30,128,128]{3,2,1,0:T(8,128)(2,1)S(1)}, bf16[1,30,128,128]{3,2,1,0:T(8,128)(2,1)}, u32[]{:S(2)}) copy-start(bf16[1,30,128,128]{3,2,1,0:T(8,128)(2,1)} %param.7) | copy-start | bytes 2949124
where the time goes:
time: 229 us; the launch traced here: 227 us
  waiting for transfers between devices  104 us (45%)
  local copies, waits for them, and re-layouts  61.3 us (27%)
  matrix products  51.4 us (22%)
  starting transfers between devices  10.8 us (5%)
    ppermute x7, waiting for transfers between devices, passed_along(): return lax.ppermute(value, axis, pairs)  104 us
    dot_general x1, local copies, waits for them, and re-layouts, per_device(): jnp.einsum('wab,kbc->kwac', left_env[0], psi, preferred_element_type=jnp....  24.5 us
    convert_element_type x1, local copies, waits for them, and re-layouts, per_device(): mixed = jnp.einsum('kwac,kwv->kavc', contracted, picked, preferred_elemen...  24.4 us
    dot_general x1, matrix products, per_device(): jnp.einsum('ko,oxb->kxb', offset_hot, stacked, preferred_element_type=jnp...  15.8 us
    dot_general x1, matrix products, per_device(): jnp.einsum('kax,kxb->kab', mixed, chosen, preferred_element_type=jnp.floa...  15 us
    dot_general x1, matrix products, per_device(): jnp.einsum('kwac,kwv->kavc', contracted, picked, preferred_element_type=j...  11.6 us
    unnamed x20, local copies, waits for them, and re-layouts  10.8 us
    ppermute x7, starting transfers between devices, passed_along(): return lax.ppermute(value, axis, pairs)  10.8 us
  transfers between devices with their start and end apart: 7, of which 3 were waited for; matrix products, arithmetic and copies ran while one was open for 36% of the time, Pallas kernels for 0%

commit v1 on v0

v1 whole, which is shorter than its diff:
```python
import functools

import jax
import jax.numpy as jnp
from jax import lax
from jax.experimental import pallas as pl
from jax.experimental.pallas import tpu as pltpu
from jax.sharding import PartitionSpec as P

SPREAD = 8
CAP = 2
LEVEL = 4
CHUNKS = 3
SUB = 8

OWN = (
    (0, 0, 1, 0), (1, 1, 1, 1), (2, 2, 1, 2), (3, 3, 1, 3),
    (2, 2, 0, 0), (3, 3, 0, 1), (1, 1, 0, 0), (3, 3, 0, 2),
)
FIRST = (
    (0, 4, 0, 2), (0, 4, 1, 1), (0, 4, 0, 1), (0, 2, 0, 1),
    (1, 5, 0, 3), (1, 5, 0, 0), (1, 3, 0, 0),
    (2, 6, 1, 3), (2, 6, 0, 0), (2, 6, 0, 3),
    (3, 7, 0, 1), (3, 7, 0, 2),
)
ACROSS = ((2, 4, 0, 3), (3, 5, 1, 2), (3, 5, 0, 2))
SECOND = (
    (1, 8, 0, 2), (0, 6, 0, 1), (1, 7, 0, 0), (2, 8, 0, 3), (2, 9, 0, 3),
)
MOVES = OWN + FIRST + ACROSS + SECOND


def kernel(
    count, bond, width, target_ref, phys_ref, psi_ref, left_ref, right_ref, mpo_ref, out_ref,
    envs, mixed, left_tiles, weights, done, order, send_sem, recv_sem, own_sem,
):
    nblock = psi_ref.shape[0]
    depth = bond * width
    part = depth // CHUNKS
    rows = bond * SUB
    padded = left_tiles.shape[1]
    group = lax.axis_index("groups")
    me = lax.axis_index("sector")
    role = lax.rem(me, LEVEL)
    base = me - role
    below = lax.rem(base + count - LEVEL, count)
    above = lax.rem(base + LEVEL, count)

    own_copy = pltpu.make_async_copy(right_ref, envs.at[0], own_sem)
    own_copy.start()

    barrier = pltpu.get_barrier_semaphore()
    for step in range(1, LEVEL):
        pl.semaphore_signal(
            barrier, inc=1, device_id=(group, base + lax.rem(role + step, LEVEL)),
            device_id_type=pl.DeviceIdType.MESH,
        )
    for place in range(LEVEL):
        for start in (below, above):
            pl.semaphore_signal(
                barrier, inc=1, device_id=(group, start + place),
                device_id_type=pl.DeviceIdType.MESH,
            )
    pl.semaphore_wait(barrier, 3 * LEVEL - 1)

    def moving(move, chunk):
        holder, i, down, target = move
        number = [m for m in MOVES if m[0] == holder].index(move)
        piece = pl.ds(chunk * part, part)
        place = i + LEVEL * down - target
        source = right_ref.at[piece] if i == holder else envs.at[i - holder, piece]
        return pltpu.make_async_remote_copy(
            src_ref=source,
            dst_ref=envs.at[place, piece],
            send_sem=send_sem.at[number, chunk],
            recv_sem=recv_sem.at[place, chunk],
            device_id=(group, (below if down else base) + target),
            device_id_type=pl.DeviceIdType.MESH,
        )

    def arrived(holder, i, chunk):
        piece = envs.at[i - holder, pl.ds(chunk * part, part)]
        pltpu.make_async_remote_copy(
            src_ref=piece,
            dst_ref=piece,
            send_sem=send_sem.at[0, chunk],
            recv_sem=recv_sem.at[i - holder, chunk],
            device_id=(group, below + holder),
            device_id_type=pl.DeviceIdType.MESH,
        ).wait_recv()

    def pass_on(moves, chunk):
        for holder in range(LEVEL):
            mine = [m for m in moves if m[0] == holder]
            if mine:

                @pl.when(role == holder)
                def _():
                    seen = set()
                    for move in mine:
                        if move[1] != holder and move[1] not in seen:
                            arrived(holder, move[1], chunk)
                        seen.add(move[1])
                        moving(move, chunk).start()

    for chunk in range(CHUNKS):
        pass_on(OWN, chunk)

    for offset in range(SPREAD):
        first = jnp.int32(nblock)
        last = jnp.int32(0)
        for k in range(nblock):
            same = target_ref[k] == offset
            first = jnp.where(same, jnp.minimum(first, k), first)
            last = jnp.where(same, k, last)
        order[CAP * offset] = jnp.minimum(first, nblock - 1)
        order[CAP * offset + 1] = last

    for tile in range(width // (2 * SUB)):
        both = left_ref[:, 2 * SUB * tile : 2 * SUB * (tile + 1), :].astype(jnp.float32)
        for half in range(2):
            slab = both[:, SUB * half : SUB * (half + 1), :].reshape(rows, width)
            left_tiles[2 * tile + half, :rows, :] = slab.astype(jnp.bfloat16)
            if padded > rows:
                left_tiles[2 * tile + half, rows:, :] = jnp.zeros(
                    (padded - rows, width), jnp.bfloat16
                )

    row_of = lax.broadcasted_iota(jnp.int32, (rows, bond), 0) // SUB
    spread_rows = (row_of == lax.broadcasted_iota(jnp.int32, (rows, bond), 1)).astype(jnp.bfloat16)
    lane_of = lax.broadcasted_iota(jnp.int32, (bond, padded), 1) // SUB
    spread_lanes = (lane_of == lax.broadcasted_iota(jnp.int32, (bond, padded), 0)).astype(
        jnp.bfloat16
    )

    def mix_pair(offset):
        blocks = [order[CAP * offset + p] for p in range(CAP)]
        for p in range(CAP):
            element = mpo_ref[phys_ref[blocks[p]]]
            tall = lax.dot_general(
                spread_rows, element, (((1,), (1,)), ((), ())),
                preferred_element_type=jnp.float32,
            ).astype(jnp.bfloat16)
            wide = jnp.dot(tall, spread_lanes, preferred_element_type=jnp.float32)
            shape = (rows, padded)
            diagonal = lax.rem(lax.broadcasted_iota(jnp.int32, shape, 0), SUB) == lax.rem(
                lax.broadcasted_iota(jnp.int32, shape, 1), SUB
            )
            weights[p] = jnp.where(diagonal, wide, 0.0).astype(jnp.bfloat16)
        both = jnp.concatenate([psi_ref[block] for block in blocks], axis=1)

        def tile_step(tile, carry):
            slabs = left_tiles[pl.ds(2 * tile, 2)].reshape(2 * padded, width)
            contracted = jnp.dot(slabs, both, preferred_element_type=jnp.float32).astype(
                jnp.bfloat16
            )
            for p in range(CAP):
                columns = slice(p * width, (p + 1) * width)
                pair = jnp.concatenate(
                    [contracted[:padded, columns], contracted[padded:, columns]], axis=1
                )
                product = jnp.dot(weights[p], pair, preferred_element_type=jnp.float32)
                tiles = jnp.concatenate(
                    [
                        product[:, :width].reshape(bond, SUB, width),
                        product[:, width:].reshape(bond, SUB, width),
                    ],
                    axis=1,
                ).astype(jnp.bfloat16)
                at = pl.ds(pl.multiple_of(p * width + tile * 2 * SUB, 2 * SUB), 2 * SUB)
                for v in range(bond):
                    mixed[offset, at, v * width : (v + 1) * width] = tiles[v]
            return carry

        lax.fori_loop(0, width // (2 * SUB), tile_step, 0)

    def mix_pairs(begin, end):
        def step(offset, carry):
            mix_pair(offset)
            return carry

        lax.fori_loop(begin, end, step, 0)

    passed = {(m[0], m[1]) for m in MOVES}

    def finish(offset):
        if offset == 0:
            own_copy.wait()
        else:
            for holder in range(LEVEL):
                if (holder, holder + offset) not in passed:

                    @pl.when(role == holder)
                    def _():
                        for chunk in range(CHUNKS):
                            arrived(holder, holder + offset, chunk)

        result = jnp.dot(mixed[offset], envs[offset], preferred_element_type=jnp.float32)
        done[pl.ds(CAP * offset, CAP)] = result.reshape(CAP, width, width).astype(jnp.bfloat16)

    mix_pairs(0, 2)
    pass_on(FIRST, 0)
    mix_pairs(2, 4)
    pass_on(FIRST, 1)
    pass_on(ACROSS, 0)
    mix_pairs(4, 6)
    pass_on(FIRST, 2)
    pass_on(ACROSS, 1)
    mix_pairs(6, SPREAD)
    pass_on(ACROSS, 2)
    finish(0)
    finish(1)
    pass_on(SECOND, 0)
    finish(2)
    finish(3)
    pass_on(SECOND, 1)
    finish(4)
    pass_on(SECOND, 2)
    for offset in range(5, SPREAD):
        finish(offset)

    for k in range(nblock):
        earlier = jnp.int32(0)
        for other in range(k):
            earlier = jnp.where(target_ref[other] == target_ref[k], 1, earlier)
        out_ref[k] = done[CAP * target_ref[k] + earlier]

    for holder in range(LEVEL):

        @pl.when(role == holder)
        def _():
            for move in MOVES:
                if move[0] == holder:
                    for chunk in range(CHUNKS):
                        moving(move, chunk).wait_send()


def per_device(count, psi, left_env, right_env, mpo, block_target, block_phys):
    nblock, width, _ = psi.shape
    bond = left_env.shape[1]
    depth = bond * width
    padded = -(-bond * SUB // 256) * 256
    sends = max(sum(m[0] == holder for m in MOVES) for holder in range(LEVEL))
    in_vmem = pl.BlockSpec(memory_space=pltpu.VMEM)
    in_smem = pl.BlockSpec(memory_space=pltpu.SMEM)
    return pl.pallas_call(
        functools.partial(kernel, count, bond, width),
        out_shape=jax.ShapeDtypeStruct((nblock, width, width), jnp.bfloat16),
        in_specs=[
            in_smem, in_smem, in_vmem, in_vmem, pl.BlockSpec(memory_space=pl.ANY), in_vmem,
        ],
        out_specs=in_vmem,
        scratch_shapes=[
            pltpu.VMEM((SPREAD, depth, width), jnp.bfloat16),
            pltpu.VMEM((SPREAD, CAP * width, depth), jnp.bfloat16),
            pltpu.VMEM((width // SUB, padded, width), jnp.bfloat16),
            pltpu.VMEM((CAP, bond * SUB, padded), jnp.bfloat16),
            pltpu.VMEM((nblock, width, width), jnp.bfloat16),
            pltpu.SMEM((CAP * SPREAD,), jnp.int32),
            pltpu.SemaphoreType.DMA((sends, CHUNKS)),
            pltpu.SemaphoreType.DMA((SPREAD, CHUNKS)),
            pltpu.SemaphoreType.DMA,
        ],
        compiler_params=pltpu.CompilerParams(
            collective_id=0, has_side_effects=True, vmem_limit_bytes=48 * 1024 * 1024
        ),
        name="hamiltonian_product",
    )(
        block_target.reshape(nblock), block_phys, psi, left_env.reshape(bond, width, width),
        right_env.reshape(depth, width), mpo,
    )


def solution(mesh):
    in_specs = (
        P(("groups", "sector"), None, None),
        P(("groups", "sector"), None, None, None),
        P(("groups", "sector"), None, None, None),
        P("groups", None, None),
        P(("groups", "sector"), None),
        P(("groups", "sector")),
    )
    out_specs = P(("groups", "sector"), None, None)
    return jax.shard_map(
        functools.partial(per_device, mesh.shape["sector"]),
        mesh=mesh, in_specs=in_specs, out_specs=out_specs, check_vma=False,
    )
```

time: 229 us -> 66.2 us (0.29)
  the two profiles are of different devices: /device:TPU:1 before, /device:TPU:3 now
where the time goes in v1:
time: 66.2 us; the launch traced here: 66 us
  Pallas kernels  60.7 us (92%)
  local copies, waits for them, and re-layouts  5.21 us (8%)
    pallas_call x1, Pallas kernels, per_device(): pl.pallas_call(functools.partial(kernel, count, bond, width), out_shape=j...  60.7 us
    unnamed x12, local copies, waits for them, and re-layouts  5.21 us

profile of v1, /device:TPU:3, one launch (start us, length us, event | category | flops | bytes accessed | tf_op | source)
XLA Modules:
  0.0 66.0 jit_solution(17808570592025562841)
XLA Ops:
  0.0 0.0 copy-start.3
  0.0 0.0 copy-start.4
  0.0 1.0 %copy.7.mpo_ref = bf16[16,30,30]{2,1,0:T(8,128)(2,1)S(1)} copy(bf16[16,30,30]{2,0,1:T(8,128)(2,1)} %param.9) | data formatting | bytes 57600 | tf_op args[3]
  1.0 0.0 copy-done.3
  1.0 0.0 copy-done.4
  1.0 0.0 copy-start
  1.0 1.2 %copy-done = bf16[1,30,128,128]{3,2,1,0:T(8,128)(2,1)S(1)} copy-done((bf16[1,30,128,128]{3,2,1,0:T(8,128)(2,1)S(1)}, bf16[1,30,128,128]{3,2,1,0:T(8,128)(2,1)}, u32[]{:S(2)}) %copy-start) | copy-done | bytes 983064
  2.2 0.0 copy-start.1
  2.2 1.2 %copy-done.1 = bf16[1,30,128,128]{3,2,1,0:T(8,128)(2,1)S(1)} copy-done((bf16[1,30,128,128]{3,2,1,0:T(8,128)(2,1)S(1)}, bf16[1,30,128,128]{3,2,1,0:T(8,128)(2,1)}, u32[]{:S(2)}) %copy-start.1) | copy-done | bytes 983064
  3.4 0.0 copy-start.2
  3.4 1.0 %copy-done.2 = bf16[16,128,128]{2,1,0:T(8,128)(2,1)S(1)} copy-done((bf16[16,128,128]{2,1,0:T(8,128)(2,1)S(1)}, bf16[16,128,128]{2,1,0:T(8,128)(2,1)}, u32[]{:S(2)}) %copy-start.2) | copy-done | bytes 524312
  4.4 60.7 %hamiltonian_product.1 = bf16[16,128,128]{2,1,0:T(8,128)(2,1)S(1)} custom-call(s32[16]{0:T(128)S(1)} %bitcast.5, s32[16]{0:T(128)S(1)} %copy-done.4, bf16[16,128,128]{2,1,0:T(8,128)(2,1)S(1)} %copy-done.2, bf16[30,128,128]{2,1,0:T(8,128)(2,1)S(1)} %bitcast.3, bf16[3840,128]{1,0:T(8,128)(2,1)S(1)} %bitcast.4, bf16[16,30,30]{2,1,0:T(8,128)(2,1)S(1)} %copy.7.mpo_ref), custom_call_target="tpu_custom_call" | custom-call | tf_op jit(solution)/shard_map/hamiltonian_product/pallas_call | solution.py:246
  65.2 0.8 %copy.9 = bf16[16,128,128]{2,1,0:T(8,128)(2,1)} copy(bf16[16,128,128]{2,1,0:T(8,128)(2,1)S(1)} %hamiltonian_product.1) | data formatting | bytes 1048576
Async XLA Ops:
  0.0 1.0 %copy-start.3 = (s32[16,1]{0,1:T(1,128)S(1)}, s32[16,1]{0,1:T(1,128)}, u32[]{:S(2)}) copy-start(s32[16,1]{0,1:T(1,128)} %param.10) | copy-start | bytes 196
  0.0 1.0 %copy-start.4 = (s32[16]{0:T(128)S(1)}, s32[16]{0:T(128)}, u32[]{:S(2)}) copy-start(s32[16]{0:T(128)} %phys_ref.1) | copy-start | bytes 196
  1.0 1.2 %copy-start = (bf16[1,30,128,128]{3,2,1,0:T(8,128)(2,1)S(1)}, bf16[1,30,128,128]{3,2,1,0:T(8,128)(2,1)}, u32[]{:S(2)}) copy-start(bf16[1,30,128,128]{3,2,1,0:T(8,128)(2,1)} %param.7) | copy-start | bytes 2949124
  2.2 1.2 %copy-start.1 = (bf16[1,30,128,128]{3,2,1,0:T(8,128)(2,1)S(1)}, bf16[1,30,128,128]{3,2,1,0:T(8,128)(2,1)}, u32[]{:S(2)}) copy-start(bf16[1,30,128,128]{3,2,1,0:T(8,128)(2,1)} %param.8) | copy-start | bytes 2949124
  3.4 1.0 %copy-start.2 = (bf16[16,128,128]{2,1,0:T(8,128)(2,1)S(1)}, bf16[16,128,128]{2,1,0:T(8,128)(2,1)}, u32[]{:S(2)}) copy-start(bf16[16,128,128]{2,1,0:T(8,128)(2,1)} %psi_ref.1) | copy-start | bytes 1572868

commit v2 on v1

--- a/solution.py
+++ b/solution.py
@@ -10,29 +10,35 @@
 SPREAD = 8
 CAP = 2
 LEVEL = 4
-CHUNKS = 3
+CHUNKS = 10
 SUB = 8
 
+ALL, EARLY, LATE = 0, 1, 2
 OWN = (
-    (0, 0, 1, 0), (1, 1, 1, 1), (2, 2, 1, 2), (3, 3, 1, 3),
-    (2, 2, 0, 0), (3, 3, 0, 1), (1, 1, 0, 0), (3, 3, 0, 2),
+    (0, 0, 1, 0, ALL), (1, 1, 1, 1, ALL), (2, 2, 1, 2, ALL), (3, 3, 1, 3, LATE),
+    (2, 2, 0, 0, ALL), (3, 3, 0, 1, ALL), (1, 1, 0, 0, ALL), (3, 3, 0, 2, ALL),
 )
 FIRST = (
-    (0, 4, 0, 2), (0, 4, 1, 1), (0, 4, 0, 1), (0, 2, 0, 1),
-    (1, 5, 0, 3), (1, 5, 0, 0), (1, 3, 0, 0),
-    (2, 6, 1, 3), (2, 6, 0, 0), (2, 6, 0, 3),
-    (3, 7, 0, 1), (3, 7, 0, 2),
+    (0, 4, 0, 2, ALL), (0, 4, 1, 1, ALL), (0, 4, 0, 1, ALL), (0, 2, 0, 1, ALL),
+    (1, 5, 0, 3, ALL), (1, 5, 0, 0, ALL), (1, 3, 1, 1, EARLY), (1, 3, 0, 0, ALL),
+    (2, 6, 0, 0, ALL), (2, 6, 1, 3, ALL), (2, 6, 0, 3, ALL),
+    (3, 7, 0, 1, LATE), (3, 7, 0, 2, LATE),
 )
-ACROSS = ((2, 4, 0, 3), (3, 5, 1, 2), (3, 5, 0, 2))
+ACROSS = ((2, 4, 0, 3, ALL), (3, 5, 1, 2, ALL), (3, 5, 0, 2, ALL))
 SECOND = (
-    (1, 8, 0, 2), (0, 6, 0, 1), (1, 7, 0, 0), (2, 8, 0, 3), (2, 9, 0, 3),
+    (1, 8, 0, 2, ALL), (1, 7, 0, 3, EARLY), (1, 7, 0, 0, ALL), (0, 6, 0, 1, ALL),
+    (2, 8, 0, 3, ALL), (2, 9, 0, 3, ALL), (3, 7, 0, 2, EARLY),
 )
 MOVES = OWN + FIRST + ACROSS + SECOND
 
 
+def applies(move, chunk):
+    return move[4] == ALL or (chunk < CHUNKS // 2) == (move[4] == EARLY)
+
+
 def kernel(
-    count, bond, width, target_ref, phys_ref, psi_ref, left_ref, right_ref, mpo_ref, out_ref,
-    envs, mixed, left_tiles, weights, done, order, send_sem, recv_sem, own_sem,
+    count, bond, width, target_ref, phys_ref, psi_hbm, left_hbm, right_ref, mpo_hbm, out_ref,
+    psi_ref, left_ref, mpo_ref, envs, mixed, left_tiles, weights, held, done, order, send_sem, recv_sem, own_sem, load_sem,
 ):
     nblock = psi_ref.shape[0]
     depth = bond * width
@@ -47,6 +53,14 @@
     above = lax.rem(base + LEVEL, count)
 
     own_copy = pltpu.make_async_copy(right_ref, envs.at[0], own_sem)
+    loads = [
+        pltpu.make_async_copy(source, target, load_sem.at[n])
+        for n, (source, target) in enumerate(
+            ((left_hbm, left_ref), (mpo_hbm, mpo_ref), (psi_hbm, psi_ref))
+        )
+    ]
+    for load in loads:
+        load.start()
     own_copy.start()
 
     barrier = pltpu.get_barrier_semaphore()
@@ -64,7 +78,7 @@
     pl.semaphore_wait(barrier, 3 * LEVEL - 1)
 
     def moving(move, chunk):
-        holder, i, down, target = move
+        holder, i, down, target, _ = move
         number = [m for m in MOVES if m[0] == holder].index(move)
         piece = pl.ds(chunk * part, part)
         place = i + LEVEL * down - target
@@ -91,7 +105,7 @@
 
     def pass_on(moves, chunk):
         for holder in range(LEVEL):
-            mine = [m for m in moves if m[0] == holder]
+            mine = [m for m in moves if m[0] == holder and applies(m, chunk)]
             if mine:
 
                 @pl.when(role == holder)
@@ -116,6 +130,9 @@
         order[CAP * offset] = jnp.minimum(first, nblock - 1)
         order[CAP * offset + 1] = last
 
+    for load in loads:
+        load.wait()
+
     for tile in range(width // (2 * SUB)):
         both = left_ref[:, 2 * SUB * tile : 2 * SUB * (tile + 1), :].astype(jnp.float32)
         for half in range(2):
@@ -133,53 +150,64 @@
         jnp.bfloat16
     )
 
-    def mix_pair(offset):
-        blocks = [order[CAP * offset + p] for p in range(CAP)]
+    shape = (rows, padded)
+    diagonal = lax.rem(lax.broadcasted_iota(jnp.int32, shape, 0), SUB) == lax.rem(
+        lax.broadcasted_iota(jnp.int32, shape, 1), SUB
+    )
+
+    def spread_element(at, carry):
+        element = mpo_ref[phys_ref[order[at]]]
+        tall = lax.dot_general(
+            spread_rows, element, (((1,), (1,)), ((), ())), preferred_element_type=jnp.float32
+        ).astype(jnp.bfloat16)
+        wide = jnp.dot(tall, spread_lanes, preferred_element_type=jnp.float32)
+        weights[at] = jnp.where(diagonal, wide, 0.0).astype(jnp.bfloat16)
+        return carry
+
+    def spread_elements(begin, end):
+        lax.fori_loop(begin, end, spread_element, 0, unroll=2)
+
+    tiles = width // (2 * SUB)
+
+    def contract(offset, tile, slot):
+        both = jnp.concatenate([psi_ref[order[CAP * offset + p]] for p in range(CAP)], axis=1)
+        slabs = left_tiles[pl.ds(2 * tile, 2)].reshape(2 * padded, width)
+        held[slot] = jnp.dot(slabs, both, preferred_element_type=jnp.float32).astype(
+            jnp.bfloat16
+        )
+
+    def mix(offset, tile, slot):
         for p in range(CAP):
-            element = mpo_ref[phys_ref[blocks[p]]]
-            tall = lax.dot_general(
-                spread_rows, element, (((1,), (1,)), ((), ())),
-                preferred_element_type=jnp.float32,
+            columns = slice(p * width, (p + 1) * width)
+            pair = jnp.concatenate(
+                [held[slot, :padded, columns], held[slot, padded:, columns]], axis=1
+            )
+            product = jnp.dot(
+                weights[CAP * offset + p], pair, preferred_element_type=jnp.float32
+            )
+            stacked = jnp.concatenate(
+                [
+                    product[:, :width].reshape(bond, SUB, width),
+                    product[:, width:].reshape(bond, SUB, width),
+                ],
+                axis=1,
             ).astype(jnp.bfloat16)
-            wide = jnp.dot(tall, spread_lanes, preferred_element_type=jnp.float32)
-            shape = (rows, padded)
-            diagonal = lax.rem(lax.broadcasted_iota(jnp.int32, shape, 0), SUB) == lax.rem(
-                lax.broadcasted_iota(jnp.int32, shape, 1), SUB
-            )
-            weights[p] = jnp.where(diagonal, wide, 0.0).astype(jnp.bfloat16)
-        both = jnp.concatenate([psi_ref[block] for block in blocks], axis=1)
-
-        def tile_step(tile, carry):
-            slabs = left_tiles[pl.ds(2 * tile, 2)].reshape(2 * padded, width)
-            contracted = jnp.dot(slabs, both, preferred_element_type=jnp.float32).astype(
-                jnp.bfloat16
-            )
-            for p in range(CAP):
-                columns = slice(p * width, (p + 1) * width)
-                pair = jnp.concatenate(
-                    [contracted[:padded, columns], contracted[padded:, columns]], axis=1
-                )
-                product = jnp.dot(weights[p], pair, preferred_element_type=jnp.float32)
-                tiles = jnp.concatenate(
-                    [
-                        product[:, :width].reshape(bond, SUB, width),
-                        product[:, width:].reshape(bond, SUB, width),
-                    ],
-                    axis=1,
-                ).astype(jnp.bfloat16)
-                at = pl.ds(pl.multiple_of(p * width + tile * 2 * SUB, 2 * SUB), 2 * SUB)
-                for v in range(bond):
-                    mixed[offset, at, v * width : (v + 1) * width] = tiles[v]
+            at = pl.ds(pl.multiple_of(p * width + tile * 2 * SUB, 2 * SUB), 2 * SUB)
+            for v in range(bond):
+                mixed[offset, at, v * width : (v + 1) * width] = stacked[v]
+
+    total_steps = SPREAD * tiles
+
+    def mix_steps(begin, end):
+        def step(n, carry):
+            for half in range(2):
+                now = 2 * n + half
+                after = jnp.minimum(now + 1, total_steps - 1)
+                contract(after // tiles, lax.rem(after, tiles), 1 - half)
+                mix(now // tiles, lax.rem(now, tiles), half)
             return carry
 
-        lax.fori_loop(0, width // (2 * SUB), tile_step, 0)
-
-    def mix_pairs(begin, end):
-        def step(offset, carry):
-            mix_pair(offset)
-            return carry
-
-        lax.fori_loop(begin, end, step, 0)
+        lax.fori_loop(begin * tiles // 4, end * tiles // 4, step, 0)
 
     passed = {(m[0], m[1]) for m in MOVES}
 
@@ -198,24 +226,28 @@
         result = jnp.dot(mixed[offset], envs[offset], preferred_element_type=jnp.float32)
         done[pl.ds(CAP * offset, CAP)] = result.reshape(CAP, width, width).astype(jnp.bfloat16)
 
-    mix_pairs(0, 2)
-    pass_on(FIRST, 0)
-    mix_pairs(2, 4)
-    pass_on(FIRST, 1)
-    pass_on(ACROSS, 0)
-    mix_pairs(4, 6)
-    pass_on(FIRST, 2)
-    pass_on(ACROSS, 1)
-    mix_pairs(6, SPREAD)
-    pass_on(ACROSS, 2)
-    finish(0)
-    finish(1)
-    pass_on(SECOND, 0)
-    finish(2)
-    finish(3)
-    pass_on(SECOND, 1)
-    finish(4)
-    pass_on(SECOND, 2)
+    def phase(n):
+        if n < CHUNKS:
+            pass_on(FIRST, n)
+        if 0 < n <= CHUNKS:
+            pass_on(ACROSS, n - 1)
+
+    spread_elements(0, CAP * SPREAD // 2)
+    phase(0)
+    spread_elements(CAP * SPREAD // 2, CAP * SPREAD)
+    contract(0, 0, 0)
+    stages = 2 * SPREAD
+    for stage in range(stages):
+        mix_steps(stage, stage + 1)
+        for n in range(1, CHUNKS + 1):
+            if (n - 1) * stages // CHUNKS == stage:
+                phase(n)
+    for chunk in range(CHUNKS):
+        pass_on(SECOND, chunk)
+        if chunk < 4:
+            finish(chunk)
+        elif chunk == CHUNKS // 2:
+            finish(4)
     for offset in range(5, SPREAD):
         finish(offset)
 
@@ -232,7 +264,8 @@
             for move in MOVES:
                 if move[0] == holder:
                     for chunk in range(CHUNKS):
-                        moving(move, chunk).wait_send()
+                        if applies(move, chunk):
+                            moving(move, chunk).wait_send()
 
 
 def per_device(count, psi, left_env, right_env, mpo, block_target, block_phys):
@@ -242,27 +275,33 @@
     padded = -(-bond * SUB // 256) * 256
     sends = max(sum(m[0] == holder for m in MOVES) for holder in range(LEVEL))
     in_vmem = pl.BlockSpec(memory_space=pltpu.VMEM)
+    in_place = pl.BlockSpec(memory_space=pl.ANY)
     in_smem = pl.BlockSpec(memory_space=pltpu.SMEM)
     return pl.pallas_call(
         functools.partial(kernel, count, bond, width),
         out_shape=jax.ShapeDtypeStruct((nblock, width, width), jnp.bfloat16),
         in_specs=[
-            in_smem, in_smem, in_vmem, in_vmem, pl.BlockSpec(memory_space=pl.ANY), in_vmem,
+            in_smem, in_smem, in_place, in_place, in_place, in_place,
         ],
         out_specs=in_vmem,
         scratch_shapes=[
+            pltpu.VMEM(psi.shape, jnp.bfloat16),
+            pltpu.VMEM((bond, width, width), jnp.bfloat16),
+            pltpu.VMEM(mpo.shape, jnp.bfloat16),
             pltpu.VMEM((SPREAD, depth, width), jnp.bfloat16),
             pltpu.VMEM((SPREAD, CAP * width, depth), jnp.bfloat16),
             pltpu.VMEM((width // SUB, padded, width), jnp.bfloat16),
-            pltpu.VMEM((CAP, bond * SUB, padded), jnp.bfloat16),
+            pltpu.VMEM((nblock, bond * SUB, padded), jnp.bfloat16),
+            pltpu.VMEM((2, 2 * padded, CAP * width), jnp.bfloat16),
             pltpu.VMEM((nblock, width, width), jnp.bfloat16),
             pltpu.SMEM((CAP * SPREAD,), jnp.int32),
             pltpu.SemaphoreType.DMA((sends, CHUNKS)),
             pltpu.SemaphoreType.DMA((SPREAD, CHUNKS)),
             pltpu.SemaphoreType.DMA,
+            pltpu.SemaphoreType.DMA((3,)),
         ],
         compiler_params=pltpu.CompilerParams(
-            collective_id=0, has_side_effects=True, vmem_limit_bytes=48 * 1024 * 1024
+            collective_id=0, has_side_effects=True, vmem_limit_bytes=60 * 1024 * 1024
         ),
         name="hamiltonian_product",
     )(

time: 66.2 us -> 58.7 us (0.89)
  Pallas kernels: 60.7 us -> 55 us
  local copies, waits for them, and re-layouts: 5.21 us -> 3.48 us
    pallas_call x1, Pallas kernels: 60.7 us -> 55 us  [per_device(): pl.pallas_call(functools.partial(kernel, count, bond, width), out_shape=j...]
    unnamed x12 -> x2, local copies, waits for them, and re-layouts: 5.21 us -> 3.48 us
where the time goes in v2:
time: 58.7 us; the launch traced here: 58.5 us
  Pallas kernels  55 us (94%)
  local copies, waits for them, and re-layouts  3.48 us (6%)
    pallas_call x1, Pallas kernels, per_device(): pl.pallas_call(functools.partial(kernel, count, bond, width), out_shape=j...  55 us
    unnamed x2, local copies, waits for them, and re-layouts  3.48 us

profile of v2, /device:TPU:3, one launch (start us, length us, event | category | flops | bytes accessed | tf_op | source)
XLA Modules:
  0.0 58.5 jit_solution(9895763701668500454)
XLA Ops:
  0.0 1.6 %copy.7.mpo_hbm = bf16[16,30,30]{2,1,0:T(8,128)(2,1)} copy(bf16[16,30,30]{2,0,1:T(8,128)(2,1)} %param.9) | data formatting | bytes 57600 | tf_op args[3]
  1.6 55.0 %hamiltonian_product.1 = bf16[16,128,128]{2,1,0:T(8,128)(2,1)} custom-call(s32[16]{0:T(128)} %bitcast.5, s32[16]{0:T(128)} %phys_ref.1, bf16[16,128,128]{2,1,0:T(8,128)(2,1)} %psi_hbm.1, bf16[30,128,128]{2,1,0:T(8,128)(2,1)} %bitcast.3, bf16[3840,128]{1,0:T(8,128)(2,1)} %bitcast.4, bf16[16,30,30]{2,1,0:T(8,128)(2,1)} %copy.7.mpo_hbm), custom_call_target="tpu_custom_call" | custom-call | tf_op jit(solution)/shard_map/hamiltonian_product/pallas_call | solution.py:280
  56.6 1.9 %copy.9 = bf16[16,128,128]{2,1,0:T(8,128)(2,1)} copy(bf16[16,128,128]{2,1,0:T(8,128)(2,1)} %hamiltonian_product.1) | data formatting | bytes 1048576
